TPU v7x, 256 devices: a whole 4x4x8 slice. The times are simulated.
256 devices in a mesh: grp: 8 (over y, core), tp: 16 (over z, x_hi), sec: 2 (over x_lo).
Axes of the slice: x: 4 (x_hi: 2, x_lo: 2; x = x_hi * 2 + x_lo), y: 4, z: 8, core: 2. Of those that a mesh axis runs over, the one named last changes fastest.
Arguments:
- layer_in: bfloat16 [2, 512, 4, 8192], P('sec', 'grp', None, 'tp'), may hold values from -6 to 6
- q_weight: bfloat16 [2, 8192, 8192], P('sec', 'grp', 'tp'), may hold values from -0.0625 to 0.0625
- kv_weight: bfloat16 [2, 8192, 2048], P('sec', 'grp', 'tp'), may hold values from -0.0625 to 0.0625
- o_weight: bfloat16 [2, 8192, 8192], P('sec', 'tp', 'grp'), may hold values from -0.5 to 0.5
- kv_cache: bfloat16 [2, 512, 4096, 256], P('sec', 'grp', 'tp'), may hold values from -600 to 600
- cache_lengths: int32 [512], P('grp'), may hold values from 1 to 512, as said below
- value_head: float32 [8192], P('tp'), may hold values from -0.0625 to 0.0625
Outputs:
- hidden_out: bfloat16 [2, 512, 4, 8192], P('sec', 'grp', None, 'tp')
- token_gap: float32 [512, 4], P('grp', 'sec')
Inputs may be any that keep to these rules, and one draw needn't show every extreme that they name: `cache_lengths`: every rollout has at least one cached position; some rollout fills the whole cache and some holds a single position. Positions at or after a rollout's length hold arbitrary values.
All inputs are finite; a program needn't handle non-finite values.
Results may differ from a plain program's by a relative error of at most 0.018.
Values may be sent and summed in bfloat16 or wider, within the bound.
A program may use at most 128 MiB of HBM per device.

v0:
```python
import jax
import jax.numpy as jnp
from jax import lax
from jax.sharding import PartitionSpec as P

KVH = 8
HD = 128
CACHE = 512


def from_partner(value, axis, bit):
    mask = 2**bit
    pairs = [(source, source ^ mask) for source in range(lax.axis_size(axis))]
    return lax.ppermute(value, axis, pairs)


def local(layer_in, q_weight, kv_weight, o_weight, kv_cache, cache_lengths, value_head):
    tp_count = lax.axis_size("tp")
    tp_place = lax.axis_index("tp")
    sec_count = lax.axis_size("sec")
    sec_place = lax.axis_index("sec")
    rollouts = layer_in.shape[1]
    new_steps = layer_in.shape[2]
    tokens = rollouts * new_steps
    local_in = layer_in[0].reshape(tokens, layer_in.shape[3])
    full_in = lax.all_gather(local_in, "tp", axis=1, tiled=True)
    query_local = q_weight[0]
    pair_local = kv_weight[0]

    def add_rows(piece):
        return jnp.dot(full_in, piece, preferred_element_type=jnp.float32)

    query_sum = add_rows(lax.all_gather(query_local, "grp", axis=0, tiled=True))
    pair_sum = add_rows(lax.all_gather(pair_local, "grp", axis=0, tiled=True))
    query_vals = query_sum.astype(jnp.bfloat16)
    pair_vals = pair_sum.astype(jnp.bfloat16)
    pair_size = max(tp_count // KVH, 1)
    is_even = tp_place % 2 == 0
    query_other, pair_other = from_partner((query_vals, pair_vals), "tp", 0)
    query_low = jnp.where(is_even, query_vals, query_other)
    query_high = jnp.where(is_even, query_other, query_vals)
    query_all = jnp.concatenate([query_low, query_high], axis=1)
    local_heads = 1
    new_key = jnp.where(is_even, pair_vals, pair_other).reshape(rollouts, new_steps, 1, HD)
    new_value = jnp.where(is_even, pair_other, pair_vals).reshape(rollouts, new_steps, 1, HD)
    groups = query_all.shape[1] // (local_heads * HD)
    query_five = query_all.reshape(rollouts, new_steps, local_heads, groups, HD)
    rows_dev = kv_cache.shape[2]
    span = rows_dev // local_heads
    start_pos = tp_place * rows_dev % CACHE
    cache_five = kv_cache[0].reshape(rollouts, local_heads, span, 2, HD)
    cache_keys = cache_five[:, :, :, 0, :]
    cache_vals = cache_five[:, :, :, 1, :]
    leader = tp_place % pair_size == 0
    visible = ((start_pos + jnp.arange(span))[None, :] < cache_lengths[:, None])[
        :, None, None, None, :
    ]
    causal = (jnp.arange(new_steps)[None, :] <= jnp.arange(new_steps)[:, None]) & leader
    causal = causal[None, :, None, None, :]
    score_scale = HD ** (-0.5)
    cache_scores = (
        jnp.einsum("rskgd,rkpd->rskgp", query_five, cache_keys, preferred_element_type=jnp.float32)
        * score_scale
    )
    new_scores = (
        jnp.einsum("rskgd,rtkd->rskgt", query_five, new_key, preferred_element_type=jnp.float32)
        * score_scale
    )
    row_peak = jnp.maximum(
        jnp.max(jnp.where(visible, cache_scores, -1e30), axis=-1),
        jnp.max(jnp.where(causal, new_scores, -1e30), axis=-1),
    )
    cache_w = jnp.where(visible, jnp.exp(cache_scores - row_peak[..., None]), 0.0)
    new_w = jnp.where(causal, jnp.exp(new_scores - row_peak[..., None]), 0.0)
    row_total = jnp.sum(cache_w, axis=-1) + jnp.sum(new_w, axis=-1)
    weighted = jnp.einsum(
        "rskgp,rkpd->rskgd",
        cache_w.astype(jnp.bfloat16),
        cache_vals,
        preferred_element_type=jnp.float32,
    )
    weighted = weighted + jnp.einsum(
        "rskgt,rtkd->rskgd",
        new_w.astype(jnp.bfloat16),
        new_value,
        preferred_element_type=jnp.float32,
    )
    own_heads = groups // 2
    low_part = (
        row_peak[:, :, :, :own_heads],
        row_total[:, :, :, :own_heads],
        weighted[:, :, :, :own_heads],
    )
    high_part = (
        row_peak[:, :, :, own_heads:],
        row_total[:, :, :, own_heads:],
        weighted[:, :, :, own_heads:],
    )
    send_part = tuple(
        (jnp.where(is_even, high_one, low_one) for low_one, high_one in zip(low_part, high_part))
    )
    keep_part = tuple(
        (jnp.where(is_even, low_one, high_one) for low_one, high_one in zip(low_part, high_part))
    )
    got_part = (
        from_partner(send_part[0].astype(jnp.bfloat16), "tp", 0).astype(jnp.float32),
        from_partner(send_part[1].astype(jnp.bfloat16), "tp", 0).astype(jnp.float32),
        from_partner(send_part[2].astype(jnp.bfloat16), "tp", 0).astype(jnp.float32),
    )
    merged_peak = jnp.maximum(keep_part[0], got_part[0])
    own_factor = jnp.exp(keep_part[0] - merged_peak)
    far_factor = jnp.exp(got_part[0] - merged_peak)
    row_total = keep_part[1] * own_factor + got_part[1] * far_factor
    weighted = keep_part[2] * own_factor[..., None] + got_part[2] * far_factor[..., None]
    context = (weighted / row_total[..., None]).astype(jnp.bfloat16).reshape(tokens, -1)
    head_terms = jnp.dot(
        context,
        lax.all_gather(o_weight[0], "grp", axis=1, tiled=True),
        preferred_element_type=jnp.float32,
    )
    result = lax.psum_scatter(
        head_terms.astype(jnp.bfloat16), "tp", scatter_dimension=1, tiled=True
    )
    other_result = from_partner(result, "sec", 0)
    policy_part = jnp.where(sec_place == 0, result, other_result).astype(jnp.float32)
    refer_part = jnp.where(sec_place == 0, other_result, result).astype(jnp.float32)
    local_gap = jnp.sum((policy_part - refer_part) * value_head, axis=1)
    token_gap = lax.psum(local_gap, "tp")
    hidden_out = result.reshape(1, rollouts, new_steps, result.shape[1])
    gap_grid = token_gap.reshape(rollouts, new_steps)
    step_share = new_steps // sec_count
    own_gap = lax.dynamic_slice_in_dim(gap_grid, sec_place * step_share, step_share, 1)
    return (hidden_out, own_gap)


def solution(mesh):
    placed = (
        P("sec", "grp", None, "tp"),
        P("sec", "grp", "tp"),
        P("sec", "grp", "tp"),
        P("sec", "tp", "grp"),
        P("sec", "grp", "tp", None),
        P("grp"),
        P("tp"),
    )
    return jax.shard_map(
        local,
        mesh=mesh,
        in_specs=placed,
        out_specs=(P("sec", "grp", None, "tp"), P("grp", "sec")),
        check_vma=False,
    )
```

profile of v0, /device:TPU:8, one launch (start us, length us, event | category | flops | bytes accessed | tf_op | source)
XLA Modules:
  0.0 563.6 jit_solution(2793352173244113551)
XLA Ops:
  7.2 0.0 all-gather.12.cloned.1.call-start
  7.2 0.7 all-gather.12.cloned.1.call-update
  7.9 0.0 all-gather.8.cloned.1.call-start
  7.9 1.7 reshape_squeeze.6
  9.7 0.0 all-gather.10.cloned.1.call-start
  9.7 0.7 all-gather.10.cloned.1.call-update
  10.4 0.0 all-gather.14.cloned.1.call-start
  10.5 0.5 all-gather.14.cloned.1.call-update
  11.0 0.0 reduce-scatter.2.cloned.1.call-start
  11.1 0.7 broadcast_compare_fusion
  11.8 27.7 %all-gather.12.cloned.1.call-done = bf16[1,8192,128]{2,1,0:T(8,128)(2,1)} async-done(((bf16[1,1024,128]{2,1,0:T(8,128)(2,1)}), bf16[1,8192,128]{2,1,0:T(8,128)(2,1)}) %all-gather.12.cloned.1.call-update) | async-done | bytes 2097168 | tf_op jit(solution)/shard_map/all_gather | solution.py:34
  39.6 109.6 %all-gather.8.cloned.1.call-done = bf16[256,8192]{1,0:T(8,128)(2,1)} async-done(((bf16[256,512]{1,0:T(8,128)(2,1)}), bf16[256,8192]{1,0:T(8,128)(2,1)}) %all-gather.8.cloned.1.call-update) | async-done | bytes 4194320 | tf_op jit(solution)/shard_map/all_gather | solution.py:26
  149.2 4.1 fusion.16
  153.3 0.6 collective-permute-start.1
  154.0 45.2 %all-gather.10.cloned.1.call-done = bf16[1,8192,512]{2,1,0:T(8,128)(2,1)} async-done(((bf16[1,1024,512]{2,1,0:T(8,128)(2,1)}), bf16[1,8192,512]{2,1,0:T(8,128)(2,1)}) %all-gather.10.cloned.1.call-update) | async-done | bytes 8388624 | tf_op jit(solution)/shard_map/all_gather | solution.py:33
  199.1 7.0 %fusion.13 = bf16[256,512]{1,0:T(8,128)(2,1)S(1)} fusion(bf16[256,8192]{1,0:T(8,128)(2,1)} %all-gather.8.cloned.1.call-done, bf16[1,8192,512]{2,1,0:T(8,128)(2,1)} %all-gather.10.cloned.1.call-done), kind=kOutput, calls=%fused_computation.22 | convolution fusion | flops 2147614720 | bytes 12845056 | tf_op jit(solution)/shard_map/dot_general | solution.py:31
  206.1 3.1 collective-permute-start
  209.2 11.7 %copy.9 = bf16[1,64,256,256]{2,3,1,0:T(8,128)(2,1)} copy(bf16[1,64,256,256]{3,2,1,0:T(8,128)(2,1)} %param.11) | data formatting | bytes 16777216 | tf_op args[4]
  221.0 0.1 maximum_bitcast_fusion
  221.0 0.1 copy.19
  221.1 2.4 select_reduce_fusion
  223.6 3.3 fusion.7
  227.0 0.5 fusion.26
  227.5 0.9 bitcast_reduce_fusion
  228.4 0.1 select_convert_fusion.1
  228.5 0.9 collective-permute-start.4
  229.5 0.1 select_convert_fusion.2
  229.6 2.8 collective-permute-start.2
  232.4 1.6 fusion.10
  234.0 0.5 fusion.11
  234.5 0.2 select_convert_fusion
  234.7 1.1 collective-permute-start.3
  235.8 0.1 collective-permute-done.2
  235.9 0.1 fusion.38
  236.0 0.2 fusion.37
  236.2 8.3 %collective-permute-done.3 = bf16[64,4,1,4,128]{4,3,1,0,2:T(4,128)(2,1)S(1)} collective-permute-done((bf16[64,4,1,4,128]{4,3,1,0,2:T(4,128)(2,1)S(1)}, bf16[64,4,1,4,128]{4,3,1,0,2:T(4,128)(2,1)S(1)}, u32[]{:S(2)}, u32[]{:S(2)}) %collective-permute-start.3) | collective-permute-done | bytes 262176 | tf_op jit(solution)/shard_map/ppermute | solution.py:14
  244.5 1.0 fusion.25
  245.4 7.9 %all-gather.14.cloned.1.call-done = bf16[1,512,8192]{2,1,0:T(8,128)(2,1)} async-done(((bf16[1,512,1024]{2,1,0:T(8,128)(2,1)}), bf16[1,512,8192]{2,1,0:T(8,128)(2,1)}) %all-gather.14.cloned.1.call-update) | async-done | bytes 8388624 | tf_op jit(solution)/shard_map/all_gather | solution.py:118
  253.3 7.7 %convolution_convert_fusion = bf16[256,8192]{1,0:T(8,128)(2,1)} fusion(bf16[1,512,8192]{2,1,0:T(8,128)(2,1)} %all-gather.14.cloned.1.call-done, bf16[32,8,4,128]{3,2,1,0:T(4,128)(2,1)S(1)} %bitcast.117), kind=kOutput, calls=%fused_computation | convolution fusion | flops 2149580800 | bytes 12845056 | tf_op jit(solution)/shard_map/dot_general | solution.py:116
  261.1 213.8 %reduce-scatter.2.cloned.1.call-done = bf16[256,512]{1,0:T(8,128)(2,1)} async-done(((bf16[256,8192]{1,0:T(8,128)(2,1)}), bf16[256,512]{1,0:T(8,128)(2,1)}) %reduce-scatter.2.cloned.1.call-update) | async-done | bytes 262160 | tf_op jit(solution)/shard_map/reduce_scatter | solution.py:121
  474.9 0.5 collective-permute-start.5
  475.4 1.8 reshape.158
  477.2 4.3 collective-permute-done.5
  481.5 1.1 multiply_reduce_fusion
  482.6 0.1 reshape.159
  482.7 73.6 %psum.7 = f32[64,4]{1,0:T(8,128)S(1)} all-reduce(f32[64,4]{1,0:T(8,128)S(1)} %reshape.159), channel_id=1, replica_groups=mesh['grp'=8,'tp'=16,'sec'=2] {'tp'}, use_global_device_ids=true, to_apply=%region_6.7 | all-reduce | flops 256 | bytes 2048 | tf_op jit(solution)/shard_map/psum | solution.py:128
  556.3 0.1 constant_dynamic-slice_fusion
  556.4 0.6 copy.12
  (18 shorter events, 0.2 us)
Async XLA Ops:
  7.2 32.4 %all-gather.12.cloned.1.call-start = ((), (), s32[]{:S(2)}) async-start(), calls=%async_computation.4 | async-start | bytes 2359296 | tf_op jit(solution)/shard_map/all_gather | solution.py:34
  7.9 141.3 %all-gather.8.cloned.1.call-start = ((), (), s32[]{:S(2)}) async-start(), calls=%async_computation.1 | async-start | bytes 4456448 | tf_op jit(solution)/shard_map/all_gather | solution.py:26
  9.7 189.4 %all-gather.10.cloned.1.call-start = ((), (), s32[]{:S(2)}) async-start(), calls=%async_computation.3 | async-start | bytes 9437184 | tf_op jit(solution)/shard_map/all_gather | solution.py:33
  10.4 242.9 %all-gather.14.cloned.1.call-start = ((), (), s32[]{:S(2)}) async-start(), calls=%async_computation.5 | async-start | bytes 9437184 | tf_op jit(solution)/shard_map/all_gather | solution.py:118
  11.0 463.9 %reduce-scatter.2.cloned.1.call-start = ((), (), s32[]{:S(2)}) async-start(), calls=%async_computation.2 | async-start | bytes 4456448 | tf_op jit(solution)/shard_map/reduce_scatter | solution.py:121
  153.3 67.6 %collective-permute-start.1 = (bf16[256,128]{1,0:T(8,128)(2,1)S(1)}, bf16[256,128]{1,0:T(8,128)(2,1)S(1)}, u32[]{:S(2)}, u32[]{:S(2)}) collective-permute-start(bf16[256,128]{1,0:T(8,128)(2,1)S(1)} %fusion.16), channel_id=1, source_target_pairs={{0,2},{2,0},{4,6},{6,4},{8,10},{10,8},{12,14},{14,12},{16,18},{18,... | collective-permute-start | bytes 196616 | tf_op jit(solution)/shard_map/ppermute | solution.py:14
  206.1 14.8 %collective-permute-start = (bf16[256,512]{1,0:T(8,128)(2,1)S(1)}, bf16[256,512]{1,0:T(8,128)(2,1)S(1)}, u32[]{:S(2)}, u32[]{:S(2)}) collective-permute-start(bf16[256,512]{1,0:T(8,128)(2,1)S(1)} %fusion.13), channel_id=1, source_target_pairs={{0,2},{2,0},{4,6},{6,4},{8,10},{10,8},{12,14},{14,12},{16,18},{18,... | collective-permute-start | bytes 786440 | tf_op jit(solution)/shard_map/ppermute | solution.py:14
  220.9 11.5 %slice-start = ((s8[8388608]{0:T(1024)(128)(4,1)}), s8[4194304]{0:T(1024)(128)(4,1)S(1)}, s32[]{:S(2)}) async-start(s8[8388608]{0:T(1024)(128)(4,1)} %bitcast.110), calls=%async_computation.6 | async-start | bytes 8388608
  223.6 8.8 %slice-start.1 = ((s8[8388608]{0:T(1024)(128)(4,1)}), s8[4194304]{0:T(1024)(128)(4,1)S(1)}, s32[]{:S(2)}) async-start(s8[8388608]{0:T(1024)(128)(4,1)} %bitcast.110), calls=%async_computation.7 | async-start | bytes 8388608
  228.5 7.5 %collective-permute-start.4 = (bf16[64,4,1,4]{3,1,0,2:T(4,128)(2,1)S(1)}, bf16[64,4,1,4]{3,1,0,2:T(4,128)(2,1)S(1)}, u32[]{:S(2)}, u32[]{:S(2)}) collective-permute-start(bf16[64,4,1,4]{3,1,0,2:T(4,128)(2,1)S(1)} %select_convert_fusion.1), channel_id=1, source_target_pairs={{0,2},{2,0},{4,6},{6,4},{8,10},{10,8},{12,14},{14,12},{16,18},{18,... | collective-permute-start | bytes 6152 | tf_op jit(solution)/shard_map/ppermute | solution.py:14
  229.6 6.3 %collective-permute-start.2 = (bf16[64,4,1,4]{3,1,0,2:T(4,128)(2,1)S(1)}, bf16[64,4,1,4]{3,1,0,2:T(4,128)(2,1)S(1)}, u32[]{:S(2)}, u32[]{:S(2)}) collective-permute-start(bf16[64,4,1,4]{3,1,0,2:T(4,128)(2,1)S(1)} %select_convert_fusion.2), channel_id=1, source_target_pairs={{0,2},{2,0},{4,6},{6,4},{8,10},{10,8},{12,14},{14,12},{16,18},{18,... | collective-permute-start | bytes 6152 | tf_op jit(solution)/shard_map/ppermute | solution.py:14
  234.7 9.8 %collective-permute-start.3 = (bf16[64,4,1,4,128]{4,3,1,0,2:T(4,128)(2,1)S(1)}, bf16[64,4,1,4,128]{4,3,1,0,2:T(4,128)(2,1)S(1)}, u32[]{:S(2)}, u32[]{:S(2)}) collective-permute-start(bf16[64,4,1,4,128]{4,3,1,0,2:T(4,128)(2,1)S(1)} %select_convert_fusion), channel_id=1, source_target_pairs={{0,2},{2,0},{4,6},{6,4},{8,10},{10,8},{12,14},{14,12},{16,18},{18,... | collective-permute-start | bytes 786440 | tf_op jit(solution)/shard_map/ppermute | solution.py:14
  261.0 220.4 %copy-start = (f32[512]{0:T(512)S(1)}, f32[512]{0:T(512)}, u32[]{:S(2)}) copy-start(f32[512]{0:T(512)} %param.13) | copy-start | bytes 6148
  474.9 6.6 %collective-permute-start.5 = (bf16[256,512]{1,0:T(8,128)(2,1)}, bf16[256,512]{1,0:T(8,128)(2,1)S(1)}, u32[]{:S(2)}, u32[]{:S(2)}) collective-permute-start(bf16[256,512]{1,0:T(8,128)(2,1)} %reduce-scatter.2.cloned.1.call-done), channel_id=1, source_target_pairs={{0,1},{1,0},{2,3},{3,2},{4,5},{5,4},{6,7},{7,6},{8,9},{9,8},{10,11... | collective-permute-start | bytes 786440 | tf_op jit(solution)/shard_map/ppermute | solution.py:14
Sparse Core Ops, SparseCore 0:
  9.9 29.6 all-gather.11
  42.6 106.5 all-gather.7
  151.1 48.0 all-gather.9
  200.8 52.4 all-gather.13
  261.2 213.6 reduce-scatter.1
where the time goes:
time: 564 us
  waiting for transfers between devices  419 us (74%)
  blocking collectives  73.6 us (13%)
  matrix products  26.7 us (5%)
  local copies, waits for them, and re-layouts  16.1 us (3%)
  between operations  14 us (2%)
  starting transfers between devices  9.26 us (2%)
    reduce_scatter x1, waiting for transfers between devices, local(): lax.psum_scatter(head_terms.astype(jnp.bfloat16), 'tp', scatter_dimension...  214 us
    all_gather x1, waiting for transfers between devices, local(): full_in = lax.all_gather(local_in, 'tp', axis=1, tiled=True)  110 us
    psum x1, blocking collectives, local(): token_gap = lax.psum(local_gap, 'tp')  73.6 us
    all_gather x1, waiting for transfers between devices, local(): query_sum = add_rows(lax.all_gather(query_local, 'grp', axis=0, tiled=True))  45.2 us
    all_gather x1, waiting for transfers between devices, local(): pair_sum = add_rows(lax.all_gather(pair_local, 'grp', axis=0, tiled=True))  27.7 us
    ppermute x6, waiting for transfers between devices, from_partner(): return lax.ppermute(value, axis, pairs)  12.6 us
    unnamed x9, local copies, waits for them, and re-layouts  12.4 us
  transfers between devices with their start and end apart: 11, of which 8 were waited for; matrix products, arithmetic and copies ran while one was open for 7% of the time, Pallas kernels for 0%

commit v1 on v0

--- a/solution.py
+++ b/solution.py
@@ -6,6 +6,19 @@
 KVH = 8
 HD = 128
 CACHE = 512
+
+
+def ring_gather(value, axis, dim):
+    ways = lax.axis_size(axis)
+    up = [(d, (d + 1) % ways) for d in range(ways)]
+    down = [(d, (d - 1) % ways) for d in range(ways)]
+    earlier, later = ([value], [value])
+    for _ in range(ways // 2):
+        earlier.append(lax.ppermute(earlier[-1], axis, up))
+    for _ in range((ways - 1) // 2):
+        later.append(lax.ppermute(later[-1], axis, down))
+    line = jnp.concatenate([*earlier[::-1], *later[1:]], axis=dim)
+    return jnp.roll(line, (lax.axis_index(axis) - ways // 2) * value.shape[dim], axis=dim)
 
 
 def from_partner(value, axis, bit):
@@ -31,7 +44,7 @@
         return jnp.dot(full_in, piece, preferred_element_type=jnp.float32)
 
     query_sum = add_rows(lax.all_gather(query_local, "grp", axis=0, tiled=True))
-    pair_sum = add_rows(lax.all_gather(pair_local, "grp", axis=0, tiled=True))
+    pair_sum = add_rows(ring_gather(pair_local, "grp", 0))
     query_vals = query_sum.astype(jnp.bfloat16)
     pair_vals = pair_sum.astype(jnp.bfloat16)
     pair_size = max(tp_count // KVH, 1)

time: 564 us -> 534 us (0.947)
  waiting for transfers between devices: 419 us -> 371 us
  local copies, waits for them, and re-layouts: 16.1 us -> 28.1 us
    all_gather x1, waiting for transfers between devices: 110 us -> 73.7 us  [local(): full_in = lax.all_gather(local_in, 'tp', axis=1, tiled=True)]
    all_gather x1 -> x0, waiting for transfers between devices: 27.7 us -> none  [local(): pair_sum = add_rows(lax.all_gather(pair_local, 'grp', axis=0, tiled=True))]
    ppermute x0 -> x7, waiting for transfers between devices: none -> 16.9 us  [the longest x4 16.7 us: ring_gather(): earlier.append(lax.ppermute(earlier[-1], axis, up))]
    unnamed x9 -> x26, local copies, waits for them, and re-layouts: 12.4 us -> 23.5 us
    ppermute x0 -> x7, starting transfers between devices: none -> 5.76 us  [the longest x3 5.73 us: ring_gather(): later.append(lax.ppermute(later[-1], axis, down))]
  transfers between devices with their start and end apart: 11 -> 17, of which waited for: 8 -> 12; matrix products, arithmetic and copies ran while one was open for 7% -> 9% of each run, Pallas kernels for 0% -> 0%
where the time goes in v1:
time: 534 us
  waiting for transfers between devices  371 us (69%)
  blocking collectives  73.6 us (14%)
  local copies, waits for them, and re-layouts  28.1 us (5%)
  matrix products  26.9 us (5%)
  starting transfers between devices  14.8 us (3%)
  between operations  14 us (3%)
    reduce_scatter x1, waiting for transfers between devices, local(): lax.psum_scatter(head_terms.astype(jnp.bfloat16), 'tp', scatter_dimension...  214 us
    all_gather x1, waiting for transfers between devices, local(): full_in = lax.all_gather(local_in, 'tp', axis=1, tiled=True)  73.7 us
    psum x1, blocking collectives, local(): token_gap = lax.psum(local_gap, 'tp')  73.6 us
    all_gather x1, waiting for transfers between devices, local(): query_sum = add_rows(lax.all_gather(query_local, 'grp', axis=0, tiled=True))  44.9 us
    unnamed x26, local copies, waits for them, and re-layouts  23.5 us
    ppermute x4, waiting for transfers between devices, ring_gather(): earlier.append(lax.ppermute(earlier[-1], axis, up))  16.7 us
    ppermute x6, waiting for transfers between devices, from_partner(): return lax.ppermute(value, axis, pairs)  12.7 us
    dot_general x2, matrix products, add_rows(): return jnp.dot(full_in, piece, preferred_element_type=jnp.float32)  11.3 us
  transfers between devices with their start and end apart: 17, of which 12 were waited for; matrix products, arithmetic and copies ran while one was open for 9% of the time, Pallas kernels for 0%

profile of v1, /device:TPU:8, one launch (start us, length us, event | category | flops | bytes accessed | tf_op | source)
XLA Modules:
  0.0 533.7 jit_solution(116871092641454850)
XLA Ops:
  7.2 1.8 reshape_squeeze.6
  9.0 0.7 all-gather.8.cloned.1.call-update
  10.6 6.0 %collective-permute-done.1 = bf16[1024,128]{1,0:T(8,128)(2,1)S(1)} collective-permute-done((bf16[1024,128]{1,0:T(8,128)(2,1)}, bf16[1024,128]{1,0:T(8,128)(2,1)S(1)}, u32[]{:S(2)}, u32[]{:S(2)}) %collective-permute-start.1) | collective-permute-done | bytes 262176 | tf_op jit(solution)/shard_map/ppermute | solution.py:17
  16.6 1.7 collective-permute-start.5
  18.3 4.1 collective-permute-done.2
  22.5 2.1 collective-permute-start.6
  24.6 3.5 collective-permute-done.3
  28.2 0.7 broadcast_compare_fusion
  28.9 1.9 collective-permute-start.7
  30.8 3.1 collective-permute-done.4
  33.9 0.7 constant_dynamic-update-slice_fusion.15
  34.7 0.7 constant_dynamic-update-slice_fusion.14
  35.4 0.7 constant_dynamic-update-slice_fusion.13
  36.1 0.7 constant_dynamic-update-slice_fusion.12
  36.9 0.7 constant_dynamic-update-slice_fusion.11
  37.6 0.7 constant_dynamic-update-slice_fusion.10
  38.3 0.7 constant_dynamic-update-slice_fusion.9
  39.1 0.7 constant_dynamic-update-slice_fusion.8
  39.8 0.7 constant_dynamic-update-slice_fusion.7
  40.5 0.7 constant_dynamic-update-slice_fusion.6
  41.3 0.7 constant_dynamic-update-slice_fusion.5
  42.0 0.7 constant_dynamic-update-slice_fusion.4
  42.7 0.7 constant_dynamic-update-slice_fusion.3
  43.4 0.7 constant_dynamic-update-slice_fusion.2
  44.1 0.7 constant_dynamic-update-slice_fusion.1
  44.9 0.7 constant_dynamic-update-slice_fusion
  45.6 73.7 %all-gather.6.cloned.1.call-done = bf16[256,8192]{1,0:T(8,128)(2,1)} async-done(((bf16[256,512]{1,0:T(8,128)(2,1)}), bf16[256,8192]{1,0:T(8,128)(2,1)}) %all-gather.6.cloned.1.call-update) | async-done | bytes 4194320 | tf_op jit(solution)/shard_map/all_gather | solution.py:39
  119.3 4.4 fusion.19
  124.3 44.9 %all-gather.8.cloned.1.call-done = bf16[1,8192,512]{2,1,0:T(8,128)(2,1)} async-done(((bf16[1,1024,512]{2,1,0:T(8,128)(2,1)}), bf16[1,8192,512]{2,1,0:T(8,128)(2,1)}) %all-gather.8.cloned.1.call-update) | async-done | bytes 8388624 | tf_op jit(solution)/shard_map/all_gather | solution.py:46
  169.2 7.0 %fusion.13 = bf16[256,512]{1,0:T(8,128)(2,1)S(1)} fusion(bf16[256,8192]{1,0:T(8,128)(2,1)} %all-gather.6.cloned.1.call-done, bf16[1,8192,512]{2,1,0:T(8,128)(2,1)} %all-gather.8.cloned.1.call-done), kind=kOutput, calls=%fused_computation.22 | convolution fusion | flops 2147614720 | bytes 12845056 | tf_op jit(solution)/shard_map/dot_general | solution.py:44
  176.2 3.1 collective-permute-start
  179.3 11.8 %copy.11 = bf16[1,64,256,256]{2,3,1,0:T(8,128)(2,1)} copy(bf16[1,64,256,256]{3,2,1,0:T(8,128)(2,1)} %param.11) | data formatting | bytes 16777216 | tf_op args[4]
  191.5 2.4 select_reduce_fusion
  194.0 3.3 fusion.5
  197.9 0.9 bitcast_reduce_fusion
  199.0 0.7 collective-permute-start.11
  199.8 3.0 collective-permute-start.9
  202.8 1.6 fusion.10
  205.1 0.9 collective-permute-start.10
  206.5 8.3 %collective-permute-done.10 = bf16[64,4,1,4,128]{4,3,1,0,2:T(4,128)(2,1)S(1)} collective-permute-done((bf16[64,4,1,4,128]{4,3,1,0,2:T(4,128)(2,1)S(1)}, bf16[64,4,1,4,128]{4,3,1,0,2:T(4,128)(2,1)S(1)}, u32[]{:S(2)}, u32[]{:S(2)}) %collective-permute-start.10) | collective-permute-done | bytes 262176 | tf_op jit(solution)/shard_map/ppermute | solution.py:27
  214.8 1.0 fusion.28
  215.7 7.8 %all-gather.10.cloned.1.call-done = bf16[1,512,8192]{2,1,0:T(8,128)(2,1)} async-done(((bf16[1,512,1024]{2,1,0:T(8,128)(2,1)}), bf16[1,512,8192]{2,1,0:T(8,128)(2,1)}) %all-gather.10.cloned.1.call-update) | async-done | bytes 8388624 | tf_op jit(solution)/shard_map/all_gather | solution.py:131
  223.6 7.7 %convolution_convert_fusion = bf16[256,8192]{1,0:T(8,128)(2,1)} fusion(bf16[1,512,8192]{2,1,0:T(8,128)(2,1)} %all-gather.10.cloned.1.call-done, bf16[32,8,4,128]{3,2,1,0:T(4,128)(2,1)S(1)} %bitcast.119), kind=kOutput, calls=%fused_computation | convolution fusion | flops 2149580800 | bytes 12845056 | tf_op jit(solution)/shard_map/dot_general | solution.py:129
  231.3 213.7 %reduce-scatter.2.cloned.1.call-done = bf16[256,512]{1,0:T(8,128)(2,1)} async-done(((bf16[256,8192]{1,0:T(8,128)(2,1)}), bf16[256,512]{1,0:T(8,128)(2,1)}) %reduce-scatter.2.cloned.1.call-update) | async-done | bytes 262160 | tf_op jit(solution)/shard_map/reduce_scatter | solution.py:134
  445.5 1.8 reshape.158
  447.3 4.3 collective-permute-done.12
  451.5 1.1 multiply_reduce_fusion
  452.8 73.6 %psum.7 = f32[64,4]{1,0:T(8,128)S(1)} all-reduce(f32[64,4]{1,0:T(8,128)S(1)} %reshape.159), channel_id=1, replica_groups=mesh['grp'=8,'tp'=16,'sec'=2] {'tp'}, use_global_device_ids=true, to_apply=%region_6.7 | all-reduce | flops 256 | bytes 2048 | tf_op jit(solution)/shard_map/psum | solution.py:141
  (49 shorter events, 5.6 us)
Async XLA Ops:
  7.2 29.7 %copy-start = (bf16[1,1024,128]{2,1,0:T(8,128)(2,1)S(1)}, bf16[1,1024,128]{2,1,0:T(8,128)(2,1)}, u32[]{:S(2)}) copy-start(bf16[1,1024,128]{2,1,0:T(8,128)(2,1)} %param.9) | copy-start | bytes 786436
  7.2 112.1 %all-gather.6.cloned.1.call-start = ((), (), s32[]{:S(2)}) async-start(), calls=%async_computation.1 | async-start | bytes 4456448 | tf_op jit(solution)/shard_map/all_gather | solution.py:39
  9.0 160.2 %all-gather.8.cloned.1.call-start = ((), (), s32[]{:S(2)}) async-start(), calls=%async_computation.3 | async-start | bytes 9437184 | tf_op jit(solution)/shard_map/all_gather | solution.py:46
  9.7 213.8 %all-gather.10.cloned.1.call-start = ((), (), s32[]{:S(2)}) async-start(), calls=%async_computation.4 | async-start | bytes 9437184 | tf_op jit(solution)/shard_map/all_gather | solution.py:131
  10.5 434.5 %reduce-scatter.2.cloned.1.call-start = ((), (), s32[]{:S(2)}) async-start(), calls=%async_computation.2 | async-start | bytes 4456448 | tf_op jit(solution)/shard_map/reduce_scatter | solution.py:134
  10.5 6.0 %collective-permute-start.1 = (bf16[1024,128]{1,0:T(8,128)(2,1)}, bf16[1024,128]{1,0:T(8,128)(2,1)S(1)}, u32[]{:S(2)}, u32[]{:S(2)}) collective-permute-start(bf16[1024,128]{1,0:T(8,128)(2,1)} %bitcast.117), channel_id=1, source_target_pairs={{0,32},{32,64},{64,96},{96,128},{128,160},{160,192},{192,224},{224... | collective-permute-start | bytes 786440 | tf_op jit(solution)/shard_map/ppermute | solution.py:17
  16.6 5.8 %collective-permute-start.2 = (bf16[1024,128]{1,0:T(8,128)(2,1)S(1)}, bf16[1024,128]{1,0:T(8,128)(2,1)S(1)}, u32[]{:S(2)}, u32[]{:S(2)}) collective-permute-start(bf16[1024,128]{1,0:T(8,128)(2,1)S(1)} %collective-permute-done.1), channel_id=1, source_target_pairs={{0,32},{32,64},{64,96},{96,128},{128,160},{160,192},{192,224},{224... | collective-permute-start | bytes 786440 | tf_op jit(solution)/shard_map/ppermute | solution.py:17
  16.6 6.0 %collective-permute-start.5 = (bf16[1024,128]{1,0:T(8,128)(2,1)}, bf16[1024,128]{1,0:T(8,128)(2,1)S(1)}, u32[]{:S(2)}, u32[]{:S(2)}) collective-permute-start(bf16[1024,128]{1,0:T(8,128)(2,1)} %bitcast.118), channel_id=1, source_target_pairs={{0,224},{32,0},{64,32},{96,64},{128,96},{160,128},{192,160},{224,1... | collective-permute-start | bytes 786440 | tf_op jit(solution)/shard_map/ppermute | solution.py:19
  22.3 5.8 %collective-permute-start.3 = (bf16[1024,128]{1,0:T(8,128)(2,1)S(1)}, bf16[1024,128]{1,0:T(8,128)(2,1)S(1)}, u32[]{:S(2)}, u32[]{:S(2)}) collective-permute-start(bf16[1024,128]{1,0:T(8,128)(2,1)S(1)} %collective-permute-done.2), channel_id=1, source_target_pairs={{0,32},{32,64},{64,96},{96,128},{128,160},{160,192},{192,224},{224... | collective-permute-start | bytes 786440 | tf_op jit(solution)/shard_map/ppermute | solution.py:17
  22.5 6.4 %collective-permute-start.6 = (bf16[1024,128]{1,0:T(8,128)(2,1)S(1)}, bf16[1024,128]{1,0:T(8,128)(2,1)S(1)}, u32[]{:S(2)}, u32[]{:S(2)}) collective-permute-start(bf16[1024,128]{1,0:T(8,128)(2,1)S(1)} %collective-permute-done.5), channel_id=1, source_target_pairs={{0,224},{32,0},{64,32},{96,64},{128,96},{160,128},{192,160},{224,1... | collective-permute-start | bytes 786440 | tf_op jit(solution)/shard_map/ppermute | solution.py:19
  28.1 5.8 %collective-permute-start.4 = (bf16[1024,128]{1,0:T(8,128)(2,1)S(1)}, bf16[1024,128]{1,0:T(8,128)(2,1)S(1)}, u32[]{:S(2)}, u32[]{:S(2)}) collective-permute-start(bf16[1024,128]{1,0:T(8,128)(2,1)S(1)} %collective-permute-done.3), channel_id=1, source_target_pairs={{0,32},{32,64},{64,96},{96,128},{128,160},{160,192},{192,224},{224... | collective-permute-start | bytes 786440 | tf_op jit(solution)/shard_map/ppermute | solution.py:17
  28.9 10.2 %collective-permute-start.7 = (bf16[1024,128]{1,0:T(8,128)(2,1)S(1)}, bf16[1024,128]{1,0:T(8,128)(2,1)S(1)}, u32[]{:S(2)}, u32[]{:S(2)}) collective-permute-start(bf16[1024,128]{1,0:T(8,128)(2,1)S(1)} %collective-permute-done.6), channel_id=1, source_target_pairs={{0,224},{32,0},{64,32},{96,64},{128,96},{160,128},{192,160},{224,1... | collective-permute-start | bytes 786440 | tf_op jit(solution)/shard_map/ppermute | solution.py:19
  123.6 67.4 %collective-permute-start.8 = (bf16[256,128]{0,1:T(8,128)(2,1)S(1)}, bf16[256,128]{0,1:T(8,128)(2,1)S(1)}, u32[]{:S(2)}, u32[]{:S(2)}) collective-permute-start(bf16[256,128]{0,1:T(8,128)(2,1)S(1)} %fusion.19), channel_id=1, source_target_pairs={{0,2},{2,0},{4,6},{6,4},{8,10},{10,8},{12,14},{14,12},{16,18},{18,... | collective-permute-start | bytes 196616 | tf_op jit(solution)/shard_map/ppermute | solution.py:27
  176.2 15.1 %collective-permute-start = (bf16[256,512]{1,0:T(8,128)(2,1)S(1)}, bf16[256,512]{1,0:T(8,128)(2,1)S(1)}, u32[]{:S(2)}, u32[]{:S(2)}) collective-permute-start(bf16[256,512]{1,0:T(8,128)(2,1)S(1)} %fusion.13), channel_id=1, source_target_pairs={{0,2},{2,0},{4,6},{6,4},{8,10},{10,8},{12,14},{14,12},{16,18},{18,... | collective-permute-start | bytes 786440 | tf_op jit(solution)/shard_map/ppermute | solution.py:27
  191.3 11.5 %slice-start = ((s8[8388608]{0:T(1024)(128)(4,1)}), s8[4194304]{0:T(1024)(128)(4,1)S(1)}, s32[]{:S(2)}) async-start(s8[8388608]{0:T(1024)(128)(4,1)} %bitcast.110), calls=%async_computation.5 | async-start | bytes 8388608
  194.0 8.8 %slice-start.1 = ((s8[8388608]{0:T(1024)(128)(4,1)}), s8[4194304]{0:T(1024)(128)(4,1)S(1)}, s32[]{:S(2)}) async-start(s8[8388608]{0:T(1024)(128)(4,1)} %bitcast.110), calls=%async_computation.6 | async-start | bytes 8388608
  199.0 7.4 %collective-permute-start.11 = (bf16[64,4,1,4]{3,1,0,2:T(4,128)(2,1)S(1)}, bf16[64,4,1,4]{3,1,0,2:T(4,128)(2,1)S(1)}, u32[]{:S(2)}, u32[]{:S(2)}) collective-permute-start(bf16[64,4,1,4]{3,1,0,2:T(4,128)(2,1)S(1)} %select_convert_fusion.1), channel_id=1, source_target_pairs={{0,2},{2,0},{4,6},{6,4},{8,10},{10,8},{12,14},{14,12},{16,18},{18,... | collective-permute-start | bytes 6152 | tf_op jit(solution)/shard_map/ppermute | solution.py:27
  199.8 6.4 %collective-permute-start.9 = (bf16[64,4,1,4]{3,1,0,2:T(4,128)(2,1)S(1)}, bf16[64,4,1,4]{3,1,0,2:T(4,128)(2,1)S(1)}, u32[]{:S(2)}, u32[]{:S(2)}) collective-permute-start(bf16[64,4,1,4]{3,1,0,2:T(4,128)(2,1)S(1)} %select_convert_fusion.2), channel_id=1, source_target_pairs={{0,2},{2,0},{4,6},{6,4},{8,10},{10,8},{12,14},{14,12},{16,18},{18,... | collective-permute-start | bytes 6152 | tf_op jit(solution)/shard_map/ppermute | solution.py:27
  205.1 9.7 %collective-permute-start.10 = (bf16[64,4,1,4,128]{4,3,1,0,2:T(4,128)(2,1)S(1)}, bf16[64,4,1,4,128]{4,3,1,0,2:T(4,128)(2,1)S(1)}, u32[]{:S(2)}, u32[]{:S(2)}) collective-permute-start(bf16[64,4,1,4,128]{4,3,1,0,2:T(4,128)(2,1)S(1)} %select_convert_fusion), channel_id=1, source_target_pairs={{0,2},{2,0},{4,6},{6,4},{8,10},{10,8},{12,14},{14,12},{16,18},{18,... | collective-permute-start | bytes 786440 | tf_op jit(solution)/shard_map/ppermute | solution.py:27
  231.3 220.3 %copy-start.1 = (f32[512]{0:T(512)S(1)}, f32[512]{0:T(512)}, u32[]{:S(2)}) copy-start(f32[512]{0:T(512)} %param.13) | copy-start | bytes 6148
  445.0 6.6 %collective-permute-start.12 = (bf16[256,512]{1,0:T(8,128)(2,1)}, bf16[256,512]{1,0:T(8,128)(2,1)S(1)}, u32[]{:S(2)}, u32[]{:S(2)}) collective-permute-start(bf16[256,512]{1,0:T(8,128)(2,1)} %reduce-scatter.2.cloned.1.call-done), channel_id=1, source_target_pairs={{0,1},{1,0},{2,3},{3,2},{4,5},{5,4},{6,7},{7,6},{8,9},{9,8},{10,11... | collective-permute-start | bytes 786440 | tf_op jit(solution)/shard_map/ppermute | solution.py:27
Sparse Core Ops, SparseCore 0:
  11.1 108.1 all-gather.5
  121.1 48.0 all-gather.7
  171.0 52.4 all-gather.9
  231.4 213.5 reduce-scatter.1
